TPU v7x, 512 devices: a whole 4x4x16 slice. The times are simulated.
512 devices in a mesh: ctx: 64 (over y, z), head: 8 (over x, core).
Axes of the slice: x: 4, y: 4, z: 16, core: 2. Of those that a mesh axis runs over, the one named last changes fastest.
Arguments:
- queries: bfloat16 [16384, 4096], P('ctx', 'head'), may hold values from -200 to 200
- span_keys: bfloat16 [16384, 4096], P('ctx', 'head'), may hold values from -6 to 6
- span_values: bfloat16 [16384, 4096], P('ctx', 'head'), may hold values from -96 to 96
- cache_keys: bfloat16 [65536, 4096], P('ctx', 'head'), may hold values from -6 to 6
- cache_values: bfloat16 [65536, 4096], P('ctx', 'head'), may hold values from -96 to 96
- land_keys: bfloat16 [1024, 4096], P('ctx', 'head'), may hold values from -4.5 to 4.5
- land_values: bfloat16 [1024, 4096], P('ctx', 'head'), may hold values from -96 to 96
- out_weight: bfloat16 [4096, 4096], P('head', 'ctx'), may hold values from -0.09375 to 0.09375
- selection: int32 [256, 32, 4], P('ctx', 'head'), may hold values from 0 to 1023, as said below
Outputs:
- projected: bfloat16 [16384, 4096], P('ctx', 'head')
Inputs may be any that keep to these rules, and one draw needn't show every extreme that they name: `selection`: the 4 blocks of one query group and head are distinct. Count block b as owned by ctx index b // 16. Over all groups and heads of one device (one index of ctx and one of head), the selections within one owner's blocks number at most 4 and form at most 1 distinct pairs of block and head; some owner receives exactly that many of both from every device.
All inputs are finite; a program needn't handle non-finite values.
Results may differ from a plain program's by a relative error of at most 0.015.
Values may be sent and summed in bfloat16 or wider, within the bound.
A program may use at most 64 MiB of HBM per device.

v0:
```python
import math
import jax
import jax.numpy as jnp
from jax import lax
from jax.sharding import Mesh
from jax.sharding import PartitionSpec as P

BLOCK = 64
CTX = ("ctx_0", "ctx_1")


def in_one_piece(arrays, axis, dim, along):
    ends, at = ([], 0)
    for a in arrays[:-1]:
        at += a.shape[along]
        ends.append(at)
    both = jnp.concatenate(arrays, axis=along)
    return tuple(jnp.split(lax.all_gather(both, axis, axis=dim, tiled=True), ends, axis=along))


def cut_along(array, dim, peers):
    before, after = (array.shape[:dim], array.shape[dim + 1 :])
    return jnp.moveaxis(array.reshape(*before, peers, -1, *after), dim, 0)


def joined_along(tiles, dim):
    shape = list(tiles.shape[1:])
    shape[dim] *= tiles.shape[0]
    return jnp.moveaxis(tiles, 0, dim).reshape(shape)


def turned_blocks(tiles, axes, turns):
    shape = [lax.axis_size(a) for a in axes]
    tiles = tiles.reshape(*shape, *tiles.shape[1:])
    for k in turns:
        tiles = lax.all_to_all(tiles, axes[k], split_axis=k, concat_axis=k, tiled=True)
    return tiles.reshape(-1, *tiles.shape[len(axes) :])


def stepwise_exchange(array, axes, turns, split_dim, concat_dim):
    tiles = cut_along(array, split_dim, lax.axis_size(axes))
    return joined_along(turned_blocks(tiles, axes, turns), concat_dim)


def gather_in_order(array, axes, turns):
    tiles = array[None]
    for k in turns:
        tiles = lax.all_gather(tiles, axes[k], axis=0, tiled=True)
    current = [lax.axis_size(axes[k]) for k in reversed(turns)]
    tiles = tiles.reshape(*current, *array.shape)
    turned = sorted(range(len(turns)), key=lambda place: turns[len(turns) - 1 - place])
    return tiles.transpose(*turned, *range(len(turns), tiles.ndim)).reshape(-1, *array.shape)


def gathered_by_axis(array, axes, turns, dim):
    return joined_along(gather_in_order(array, axes, turns), dim)


def sum_at_owner(array, axis, dim):
    peers = lax.axis_size(axis)
    tiles = lax.all_to_all(cut_along(array, dim, peers), axis, 0, 0, tiled=True)
    return jnp.sum(tiles.astype(jnp.float32), axis=0)


def local(
    queries,
    span_keys,
    span_values,
    cache_keys,
    cache_values,
    land_keys,
    land_values,
    out_weight,
    selection,
):
    query_rows, row_width = queries.shape
    groups, head_dev, pick_count = selection.shape
    head_size = row_width // head_dev
    blocks_dev = cache_keys.shape[0] // BLOCK
    devices = lax.axis_size(CTX)
    scaling = 1.0 / math.sqrt(head_size)
    query_heads = queries.reshape(query_rows, head_dev, head_size)
    pieces = in_one_piece((land_keys, land_values), CTX, 0, 1)
    run_max = jnp.full((head_dev, query_rows), -jnp.inf, jnp.float32)
    run_sum = jnp.zeros((head_dev, query_rows), jnp.float32)
    run_acc = jnp.zeros((head_dev, query_rows, head_size), jnp.float32)
    key_piece = pieces[0].reshape(-1, head_dev, head_size)
    value_piece = pieces[1].reshape(-1, head_dev, head_size)
    scores = (
        jnp.einsum("qhd,nhd->hqn", query_heads, key_piece, preferred_element_type=jnp.float32)
        * scaling
    )
    new_max = jnp.max(scores, axis=2)
    weights = jnp.exp(scores - new_max[:, :, None])
    factor = jnp.exp(run_max - new_max)
    new_sum = run_sum * factor + jnp.sum(weights, axis=2)
    new_acc = run_acc * factor[:, :, None] + jnp.einsum(
        "hqn,nhd->hqd",
        weights.astype(jnp.bfloat16),
        value_piece,
        preferred_element_type=jnp.float32,
    )
    request_count = groups * head_dev * pick_count
    owners_flat = (selection // blocks_dev).reshape(request_count)
    block_flat = (selection % blocks_dev).reshape(request_count)
    head_flat = jnp.broadcast_to(
        jnp.arange(head_dev, dtype=jnp.int32)[None, :, None], selection.shape
    ).reshape(request_count)
    request_order = jnp.arange(request_count)
    earlier = request_order[None, :] < request_order[:, None]
    same_owner = owners_flat[:, None] == owners_flat[None, :]
    distinct_most = (head_dev * 2 * pick_count + devices - 1) // devices
    key_blocks = cache_keys.reshape(blocks_dev, BLOCK, head_dev, head_size)
    value_blocks = cache_values.reshape(blocks_dev, BLOCK, head_dev, head_size)
    asked_pairs = jnp.stack([block_flat, head_flat], axis=1)
    pair_ids = selection.reshape(request_count) * head_dev + head_flat
    same_pair = pair_ids[:, None] == pair_ids[None, :]
    is_first = jnp.logical_not(jnp.any(same_pair & earlier, axis=1))
    first_rank = jnp.sum(same_owner & earlier & is_first[None, :], axis=1)
    slot_ids = jnp.sum(jnp.where(same_pair & is_first[None, :], first_rank[None, :], 0), axis=1)
    wanted = (
        jnp.zeros((devices, distinct_most, 2), jnp.int32).at[owners_flat, slot_ids].set(asked_pairs)
    )
    asked_for = stepwise_exchange(wanted, CTX, (0, 1), 0, 0)
    sent_keys = key_blocks[asked_for[:, :, 0], :, asked_for[:, :, 1], :]
    sent_values = value_blocks[asked_for[:, :, 0], :, asked_for[:, :, 1], :]
    fetched_keys = lax.all_to_all(sent_keys, CTX, split_axis=0, concat_axis=0, tiled=True)
    fetched_values = lax.all_to_all(sent_values, CTX, split_axis=0, concat_axis=0, tiled=True)
    owner_grid = owners_flat.reshape(selection.shape)
    slot_grid = slot_ids.reshape(selection.shape)
    chosen_keys = fetched_keys[owner_grid, slot_grid]
    chosen_values = fetched_values[owner_grid, slot_grid].reshape(
        groups, head_dev, pick_count * BLOCK, head_size
    )
    query_groups = query_heads.reshape(groups, BLOCK, head_dev, head_size)
    chosen_scores = (
        jnp.einsum(
            "gqhd,ghpkd->ghqpk", query_groups, chosen_keys, preferred_element_type=jnp.float32
        )
        * scaling
    )
    chosen_scores = chosen_scores.reshape(groups, head_dev, BLOCK, pick_count * BLOCK)
    local_keys = span_keys.reshape(groups, BLOCK, head_dev, head_size)
    local_values = span_values.reshape(groups, BLOCK, head_dev, head_size)
    causal = jnp.arange(BLOCK)[:, None] >= jnp.arange(BLOCK)[None, :]
    local_scores = (
        jnp.einsum("gqhd,gkhd->ghqk", query_groups, local_keys, preferred_element_type=jnp.float32)
        * scaling
    )
    local_scores = jnp.where(causal[None, None], local_scores, -jnp.inf)
    land_top = jnp.transpose(new_max.reshape(head_dev, groups, BLOCK), (1, 0, 2))
    land_total = jnp.transpose(new_sum.reshape(head_dev, groups, BLOCK), (1, 0, 2))
    land_part = jnp.transpose(new_acc.reshape(head_dev, groups, BLOCK, head_size), (1, 0, 2, 3))
    overall_top = jnp.maximum(
        jnp.maximum(land_top, jnp.max(chosen_scores, axis=3)), jnp.max(local_scores, axis=3)
    )
    land_weight = jnp.exp(land_top - overall_top)
    chosen_weights = jnp.exp(chosen_scores - overall_top[..., None])
    local_weights = jnp.exp(local_scores - overall_top[..., None])
    denominator = (
        land_total * land_weight + jnp.sum(chosen_weights, axis=3) + jnp.sum(local_weights, axis=3)
    )
    numerator = land_part * land_weight[..., None]
    numerator = numerator + jnp.einsum(
        "ghqn,ghnd->ghqd",
        chosen_weights.astype(jnp.bfloat16),
        chosen_values,
        preferred_element_type=jnp.float32,
    )
    numerator = numerator + jnp.einsum(
        "ghqk,gkhd->ghqd",
        local_weights.astype(jnp.bfloat16),
        local_values,
        preferred_element_type=jnp.float32,
    )
    attended = (numerator / denominator[..., None]).astype(jnp.bfloat16)
    attended = jnp.transpose(attended, (0, 2, 1, 3)).reshape(query_rows, row_width)
    partial_out = jnp.dot(
        attended, gathered_by_axis(out_weight, CTX, (0, 1), 1), preferred_element_type=jnp.float32
    )
    summed = sum_at_owner(partial_out.astype(jnp.bfloat16), "head", 1)
    return summed.astype(jnp.bfloat16)


def solution(mesh):
    torus = Mesh(mesh.devices.reshape(4, 16, mesh.shape["head"]), ("ctx_0", "ctx_1", "head"))
    in_specs = (
        P(CTX, "head"),
        P(CTX, "head"),
        P(CTX, "head"),
        P(CTX, "head"),
        P(CTX, "head"),
        P(CTX, "head"),
        P(CTX, "head"),
        P("head", CTX),
        P(CTX, "head", None),
    )
    out_specs = P(CTX, "head")
    return jax.shard_map(local, mesh=torus, in_specs=in_specs, out_specs=out_specs, check_vma=False)
```

profile of v0, /device:TPU:1, one launch (start us, length us, event | category | flops | bytes accessed | tf_op | source)
XLA Modules:
  0.0 299.0 jit_solution(17440961947433692486)
XLA Ops:
  6.5 1.3 pad_maximum_fusion
  10.7 8.9 %all_to_all.25 = s32[4,16,1,1,2]{1,4,3,2,0:T(2,128)S(1)} all-to-all(s32[4,16,1,1,2]{1,4,3,2,0:T(2,128)S(1)} %copy.167), channel_id=1, replica_groups=mesh['ctx_0'=4,'ctx_1'=16,'head'=8] {'ctx_0'}, dimensions={0} | all-to-all | bytes 1024 | tf_op jit(solution)/shard_map/all_to_all | solution.py:36
  20.3 14.9 %all-to-all-start.1 = ((s32[4,16,1,1,2]{0,4,3,2,1:T(2,128)}), s32[4,16,1,1,2]{0,4,3,2,1:T(2,128)S(1)}, u32[]{:S(2)}, u32[]{:S(2)}) async-start(s32[4,16,1,1,2]{0,4,3,2,1:T(2,128)} %copy.168), calls=%async_computation.1 | async-start | bytes 32768 | tf_op jit(solution)/shard_map/all_to_all | solution.py:36
  35.2 1.4 reshape.202
  36.9 9.7 %all-to-all-done.1 = s32[4,16,1,1,2]{0,4,3,2,1:T(2,128)S(1)} async-done(((s32[4,16,1,1,2]{0,4,3,2,1:T(2,128)}), s32[4,16,1,1,2]{0,4,3,2,1:T(2,128)S(1)}, u32[]{:S(2)}, u32[]{:S(2)}) %all-to-all-start.1) | async-done | bytes 544 | tf_op jit(solution)/shard_map/all_to_all | solution.py:36
  46.8 1.7 gather_fusion
  48.6 4.7 %all-to-all-start.2 = ((bf16[64,1,64,128]{3,2,1,0:T(8,128)(2,1)}), bf16[64,1,64,128]{3,2,1,0:T(8,128)(2,1)S(1)}, u32[]{:S(2)}, u32[]{:S(2)}) async-start(bf16[64,1,64,128]{3,2,1,0:T(8,128)(2,1)} %bitcast.12), calls=%async_computation.2 | async-start | bytes 2097152 | tf_op jit(solution)/shard_map/all_to_all | solution.py:127
  53.3 10.7 %all-gather = bf16[2048,64]{0,1:T(8,128)(2,1)S(1)} all-gather(bf16[512,64]{0,1:T(8,128)(2,1)S(1)} %copy-done.5), channel_id=2, replica_groups=mesh['ctx_0'=4,'ctx_1'=16,'head'=8] {'ctx_0'}, dimensions={0}, use_global_device_ids=true | all-gather | bytes 327680 | tf_op jit(solution)/shard_map/all_gather | solution.py:48
  65.3 1.8 gather_fusion.2
  67.1 35.5 %all-to-all-done.2 = bf16[64,1,64,128]{3,2,1,0:T(8,128)(2,1)S(1)} async-done(((bf16[64,1,64,128]{3,2,1,0:T(8,128)(2,1)}), bf16[64,1,64,128]{3,2,1,0:T(8,128)(2,1)S(1)}, u32[]{:S(2)}, u32[]{:S(2)}) %all-to-all-start.2) | async-done | bytes 1048608 | tf_op jit(solution)/shard_map/all_to_all | solution.py:127
  102.6 11.2 %all-to-all-start.3 = ((bf16[64,1,64,128]{3,2,1,0:T(8,128)(2,1)}), bf16[64,1,64,128]{3,2,1,0:T(8,128)(2,1)S(1)}, u32[]{:S(2)}, u32[]{:S(2)}) async-start(bf16[64,1,64,128]{3,2,1,0:T(8,128)(2,1)} %bitcast.22), calls=%async_computation.3 | async-start | bytes 2097152 | tf_op jit(solution)/shard_map/all_to_all | solution.py:128
  114.1 1.1 reshape.206
  115.3 1.7 reshape.210
  117.0 1.1 fusion.50
  118.1 56.2 %all-gather.4.cloned.1.call-done = bf16[1024,1024]{1,0:T(8,128)(2,1)} async-done(((bf16[16,1024]{1,0:T(8,128)(2,1)}), bf16[1024,1024]{1,0:T(8,128)(2,1)}) %all-gather.4.cloned.1.call-update) | async-done | bytes 2097168 | tf_op jit(solution)/shard_map/all_gather | solution.py:18
  174.3 2.7 fusion.49
  177.0 2.3 copy.196
  179.2 4.0 %bitcast_reduce_fusion = (f32[4,256]{1,0:T(4,128)S(1)}, f32[4,1024,256]{2,1,0:T(8,128)}) fusion(bf16[1024,4,128]{0,2,1:T(8,128)(2,1)} %bitcast.142, bf16[256,512]{1,0:T(8,128)(2,1)S(1)} %copy-done), kind=kOutput, calls=%fused_computation.7 | convolution fusion | flops 270531584 | bytes 5509120 | tf_op jit(solution)/shard_map/qhd,nhd->hqn/dot_general | solution.py:90
  183.3 2.9 fusion.1
  186.2 1.3 copy.197
  187.5 4.4 %fusion.11 = f32[4,256,128]{2,1,0:T(8,128)} fusion(bf16[1024,4,128]{0,2,1:T(8,128)(2,1)} %bitcast.141, f32[4,1024,256]{2,1,0:T(8,128)} %get-tuple-element.19, f32[4,256]{1,0:T(4,128)S(1)} %get-tuple-element.18, f32[4,256]{1,0:T(4,128)S(1)} %exponential_multiply_fusion), kind=kOutput, calls=%fused_computation.24 | convolution fusion | flops 271712256 | bytes 5775360 | tf_op jit(solution)/shard_map/hqn,nhd->hqd/dot_general | solution.py:97
  191.9 1.7 gather_fusion.1
  193.6 1.7 bitcast_reduce_fusion.1
  195.3 1.6 copy.176
  196.8 1.7 gather_fusion.3
  198.6 1.2 fusion.18
  200.1 1.3 convolution_bitcast_fusion
  201.5 2.2 fusion.16
  203.9 42.9 %all-gather.6.cloned.1.call-done = bf16[64,512,64]{1,2,0:T(8,128)(2,1)} async-done(((bf16[4,512,64]{1,2,0:T(8,128)(2,1)}), bf16[64,512,64]{1,2,0:T(8,128)(2,1)}) %all-gather.6.cloned.1.call-update) | async-done | bytes 4194320 | tf_op jit(solution)/shard_map/all_gather | solution.py:48
  246.8 2.7 copy.185
  249.5 1.3 convolution_convert_fusion
  251.0 40.1 %all_to_all.26 = bf16[8,256,512]{2,1,0:T(8,128)(2,1)S(1)} all-to-all(bf16[8,256,512]{2,1,0:T(8,128)(2,1)S(1)} %bitcast.138), channel_id=1, replica_groups=mesh['ctx_0'=4,'ctx_1'=16,'head'=8] {'head'}, dimensions={0} | all-to-all | bytes 4194304 | tf_op jit(solution)/shard_map/all_to_all | solution.py:61
  (57 shorter events, 7.5 us)
Async XLA Ops:
  6.5 167.7 %all-gather.4.cloned.1.call-start = ((), (), s32[]{:S(2)}) async-start(), calls=%async_computation.5 | async-start | bytes 2129920 | tf_op jit(solution)/shard_map/all_gather | solution.py:18
  20.3 26.3 %all-to-all-start.1 = ((s32[4,16,1,1,2]{0,4,3,2,1:T(2,128)}), s32[4,16,1,1,2]{0,4,3,2,1:T(2,128)S(1)}, u32[]{:S(2)}, u32[]{:S(2)}) async-start(s32[4,16,1,1,2]{0,4,3,2,1:T(2,128)} %copy.168), calls=%async_computation.1 | async-start | bytes 32768 | tf_op jit(solution)/shard_map/all_to_all | solution.py:36
  35.2 18.1 %copy-start.5 = (bf16[512,64]{0,1:T(8,128)(2,1)S(1)}, bf16[512,64]{0,1:T(8,128)(2,1)}, u32[]{:S(2)}) copy-start(bf16[512,64]{0,1:T(8,128)(2,1)} %param.16) | copy-start | bytes 196612
  36.9 27.8 %copy-start.2 = (bf16[1024,512]{1,0:T(8,128)(2,1)S(1)}, bf16[1024,512]{1,0:T(8,128)(2,1)}, u32[]{:S(2)}) copy-start(bf16[1024,512]{1,0:T(8,128)(2,1)} %param.13) | copy-start | bytes 3145732
  48.6 54.0 %all-to-all-start.2 = ((bf16[64,1,64,128]{3,2,1,0:T(8,128)(2,1)}), bf16[64,1,64,128]{3,2,1,0:T(8,128)(2,1)S(1)}, u32[]{:S(2)}, u32[]{:S(2)}) async-start(bf16[64,1,64,128]{3,2,1,0:T(8,128)(2,1)} %bitcast.12), calls=%async_computation.2 | async-start | bytes 2097152 | tf_op jit(solution)/shard_map/all_to_all | solution.py:127
  53.2 193.6 %all-gather.6.cloned.1.call-start = ((), (), s32[]{:S(2)}) async-start(), calls=%async_computation.6 | async-start | bytes 4456448 | tf_op jit(solution)/shard_map/all_gather | solution.py:48
  64.7 49.3 %copy-start = (bf16[256,512]{1,0:T(8,128)(2,1)S(1)}, bf16[256,512]{1,0:T(8,128)(2,1)}, u32[]{:S(2)}) copy-start(bf16[256,512]{1,0:T(8,128)(2,1)} %param.9) | copy-start | bytes 786436
  102.6 94.3 %all-to-all-start.3 = ((bf16[64,1,64,128]{3,2,1,0:T(8,128)(2,1)}), bf16[64,1,64,128]{3,2,1,0:T(8,128)(2,1)S(1)}, u32[]{:S(2)}, u32[]{:S(2)}) async-start(bf16[64,1,64,128]{3,2,1,0:T(8,128)(2,1)} %bitcast.22), calls=%async_computation.3 | async-start | bytes 2097152 | tf_op jit(solution)/shard_map/all_to_all | solution.py:128
  114.1 4.0 %copy-start.3 = (bf16[4,64,4,128]{3,2,1,0:T(4,128)(2,1)}, bf16[4,64,4,128]{3,2,1,0:T(4,128)(2,1)S(1)}, u32[]{:S(2)}) copy-start(bf16[4,64,4,128]{3,2,1,0:T(4,128)(2,1)S(1)} %reshape_reshape.11) | copy-start | bytes 786436
  187.5 6.1 %copy-start.4 = (bf16[4,64,4,128]{3,2,1,0:T(4,128)(2,1)S(1)}, bf16[4,64,4,128]{3,2,1,0:T(4,128)(2,1)}, u32[]{:S(2)}) copy-start(bf16[4,64,4,128]{3,2,1,0:T(4,128)(2,1)} %copy-done.3) | copy-start | bytes 786436
  195.3 4.9 %copy-start.1 = (bf16[4,64,4,128]{3,2,1,0:T(4,128)(2,1)S(1)}, bf16[4,64,4,128]{3,2,1,0:T(4,128)(2,1)}, u32[]{:S(2)}) copy-start(bf16[4,64,4,128]{3,2,1,0:T(4,128)(2,1)} %reshape.210) | copy-start | bytes 786436
Sparse Core Ops, SparseCore 0:
  10.3 163.9 all-gather.3
  176.4 70.4 all-gather.5
where the time goes:
time: 300 us; the launch traced here: 299 us
  waiting for transfers between devices  144 us (48%)
  blocking collectives  59.7 us (20%)
  starting transfers between devices  30.9 us (10%)
  local copies, waits for them, and re-layouts  26.3 us (9%)
  matrix products  15.9 us (5%)
  between operations  13.7 us (5%)
  other arithmetic  8.18 us (3%)
    all_gather x1, waiting for transfers between devices, in_one_piece(): lax.all_gather(both, axis, axis=dim, tiled=True)  56.2 us
    all_gather x1, waiting for transfers between devices, gather_in_order(): tiles = lax.all_gather(tiles, axes[k], axis=0, tiled=True)  42.9 us
    all_to_all x1, blocking collectives, sum_at_owner(): tiles = lax.all_to_all(cut_along(array, dim, peers), axis, 0, 0, tiled=True)  40.1 us
    all_to_all x1, waiting for transfers between devices, local(): lax.all_to_all(sent_keys, CTX, split_axis=0, concat_axis=0, tiled=True)  35.5 us
    all_to_all x1, starting transfers between devices, turned_blocks(): lax.all_to_all(tiles, axes[k], split_axis=k, concat_axis=k, tiled=True)  14.9 us
    all_to_all x1, starting transfers between devices, local(): lax.all_to_all(sent_values, CTX, split_axis=0, concat_axis=0, tiled=True)  11.2 us
    all_gather x1, blocking collectives, gather_in_order(): tiles = lax.all_gather(tiles, axes[k], axis=0, tiled=True)  10.7 us
    all_to_all x1, waiting for transfers between devices, turned_blocks(): lax.all_to_all(tiles, axes[k], split_axis=k, concat_axis=k, tiled=True)  9.71 us
  transfers between devices with their start and end apart: 5, of which 4 were waited for; matrix products, arithmetic and copies ran while one was open for 15% of the time, Pallas kernels for 0%

commit v1 on v0

--- a/solution.py
+++ b/solution.py
@@ -45,7 +45,9 @@
 def gather_in_order(array, axes, turns):
     tiles = array[None]
     for k in turns:
-        tiles = lax.all_gather(tiles, axes[k], axis=0, tiled=True)
+        tiles = jnp.concatenate(
+            lax.all_to_all(jnp.stack([tiles] * lax.axis_size(axes[k])), axes[k], 0, 0), axis=0
+        )
     current = [lax.axis_size(axes[k]) for k in reversed(turns)]
     tiles = tiles.reshape(*current, *array.shape)
     turned = sorted(range(len(turns)), key=lambda place: turns[len(turns) - 1 - place])

time: 300 us -> 464 us (1.55)
  waiting for transfers between devices: 144 us -> 261 us
  blocking collectives: 59.7 us -> 103 us
    all_gather x1, waiting for transfers between devices: 56.2 us -> 203 us  [in_one_piece(): lax.all_gather(both, axis, axis=dim, tiled=True)]
    all_to_all x0 -> x1, blocking collectives: none -> 59.1 us  [local(): lax.all_to_all(sent_values, CTX, split_axis=0, concat_axis=0, tiled=True)]
    all_gather x1 -> x0, waiting for transfers between devices: 42.9 us -> none  [gather_in_order(): tiles = lax.all_gather(tiles, axes[k], axis=0, tiled=True)]
    all_gather x1 -> x0, blocking collectives: 10.7 us -> none  [gather_in_order(): tiles = lax.all_gather(tiles, axes[k], axis=0, tiled=True)]
    all_to_all x1, waiting for transfers between devices: 35.5 us -> 44.8 us  [local(): lax.all_to_all(sent_keys, CTX, split_axis=0, concat_axis=0, tiled=True)]
    all_to_all x1, blocking collectives: 40.1 us -> 34.7 us  [sum_at_owner(): tiles = lax.all_to_all(cut_along(array, dim, peers), axis, 0, 0, tiled=True)]
    all_to_all x1 -> x2, starting transfers between devices: 11.2 us -> 12.5 us  [gather_in_order(): lax.all_to_all(jnp.stack([tiles] * lax.axis_size(axes[k])), axes[k], 0, 0)]
  transfers between devices with their start and end apart: 5 -> 5, of which waited for: 4 -> 4; matrix products, arithmetic and copies ran while one was open for 15% -> 9% of each run, Pallas kernels for 0% -> 0%
where the time goes in v1:
time: 464 us; the launch traced here: 462 us
  waiting for transfers between devices  261 us (56%)
  blocking collectives  103 us (22%)
  starting transfers between devices  32.3 us (7%)
  local copies, waits for them, and re-layouts  28.2 us (6%)
  matrix products  16.9 us (4%)
  between operations  13.7 us (3%)
  other arithmetic  7.46 us (2%)
    all_gather x1, waiting for transfers between devices, in_one_piece(): lax.all_gather(both, axis, axis=dim, tiled=True)  203 us
    all_to_all x1, blocking collectives, local(): lax.all_to_all(sent_values, CTX, split_axis=0, concat_axis=0, tiled=True)  59.1 us
    all_to_all x1, waiting for transfers between devices, local(): lax.all_to_all(sent_keys, CTX, split_axis=0, concat_axis=0, tiled=True)  44.8 us
    all_to_all x1, blocking collectives, sum_at_owner(): tiles = lax.all_to_all(cut_along(array, dim, peers), axis, 0, 0, tiled=True)  34.7 us
    all_to_all x1, starting transfers between devices, turned_blocks(): lax.all_to_all(tiles, axes[k], split_axis=k, concat_axis=k, tiled=True)  14.9 us
    all_to_all x2, starting transfers between devices, gather_in_order(): lax.all_to_all(jnp.stack([tiles] * lax.axis_size(axes[k])), axes[k], 0, 0)  12.5 us
    all_to_all x1, waiting for transfers between devices, turned_blocks(): lax.all_to_all(tiles, axes[k], split_axis=k, concat_axis=k, tiled=True)  9.66 us
  transfers between devices with their start and end apart: 5, of which 4 were waited for; matrix products, arithmetic and copies ran while one was open for 9% of the time, Pallas kernels for 0%

profile of v1, /device:TPU:1, one launch (start us, length us, event | category | flops | bytes accessed | tf_op | source)
XLA Modules:
  0.0 461.9 jit_solution(18258083947513835523)
XLA Ops:
  9.3 8.9 %all_to_all.35 = s32[4,16,1,1,2]{1,4,3,2,0:T(2,128)S(1)} all-to-all(s32[4,16,1,1,2]{1,4,3,2,0:T(2,128)S(1)} %copy.138), channel_id=1, replica_groups=mesh['ctx_0'=4,'ctx_1'=16,'head'=8] {'ctx_0'}, dimensions={0} | all-to-all | bytes 1024 | tf_op jit(solution)/shard_map/all_to_all | solution.py:36
  19.0 14.9 %all-to-all-start.1 = ((s32[4,16,1,1,2]{0,4,3,2,1:T(2,128)}), s32[4,16,1,1,2]{0,4,3,2,1:T(2,128)S(1)}, u32[]{:S(2)}, u32[]{:S(2)}) async-start(s32[4,16,1,1,2]{0,4,3,2,1:T(2,128)} %copy.139), calls=%async_computation.1 | async-start | bytes 32768 | tf_op jit(solution)/shard_map/all_to_all | solution.py:36
  33.9 1.4 reshape.203
  35.6 9.7 %all-to-all-done.1 = s32[4,16,1,1,2]{0,4,3,2,1:T(2,128)S(1)} async-done(((s32[4,16,1,1,2]{0,4,3,2,1:T(2,128)}), s32[4,16,1,1,2]{0,4,3,2,1:T(2,128)S(1)}, u32[]{:S(2)}, u32[]{:S(2)}) %all-to-all-start.1) | async-done | bytes 544 | tf_op jit(solution)/shard_map/all_to_all | solution.py:36
  46.0 3.4 all-to-all-start.4
  49.6 1.7 gather_fusion
  51.4 3.6 all-to-all-done.4
  54.9 4.7 %all-to-all-start.2 = ((bf16[64,1,64,128]{3,2,1,0:T(8,128)(2,1)}), bf16[64,1,64,128]{3,2,1,0:T(8,128)(2,1)S(1)}, u32[]{:S(2)}, u32[]{:S(2)}) async-start(bf16[64,1,64,128]{3,2,1,0:T(8,128)(2,1)} %bitcast.12), calls=%async_computation.2 | async-start | bytes 2097152 | tf_op jit(solution)/shard_map/all_to_all | solution.py:129
  61.0 44.8 %all-to-all-done.2 = bf16[64,1,64,128]{3,2,1,0:T(8,128)(2,1)S(1)} async-done(((bf16[64,1,64,128]{3,2,1,0:T(8,128)(2,1)}), bf16[64,1,64,128]{3,2,1,0:T(8,128)(2,1)S(1)}, u32[]{:S(2)}, u32[]{:S(2)}) %all-to-all-start.2) | async-done | bytes 1048608 | tf_op jit(solution)/shard_map/all_to_all | solution.py:129
  105.7 59.1 %all_to_all.36 = bf16[64,1,64,128]{3,2,1,0:T(8,128)(2,1)S(1)} all-to-all(bf16[64,1,64,128]{3,2,1,0:T(8,128)(2,1)S(1)} %bitcast.135), channel_id=1, replica_groups=mesh['ctx_0'=4,'ctx_1'=16,'head'=8] {'ctx_0','ctx_1'}, dimensions={0} | all-to-all | bytes 2097152 | tf_op jit(solution)/shard_map/all_to_all | solution.py:130
  164.8 2.5 stack.11
  167.3 9.1 %all-to-all-start.5 = ((bf16[16,4,512,64]{2,3,1,0:T(8,128)(2,1)}), bf16[16,4,512,64]{2,3,1,0:T(8,128)(2,1)}, u32[]{:S(2)}, u32[]{:S(2)}) async-start(bf16[16,4,512,64]{2,3,1,0:T(8,128)(2,1)} %stack.11), calls=%async_computation.5 | async-start | bytes 8388608 | tf_op jit(solution)/shard_map/all_to_all | solution.py:49
  178.3 1.0 reshape.211
  179.4 2.0 fusion.50
  181.4 202.7 %all-gather.2.cloned.1.call-done = bf16[1024,1024]{1,0:T(8,128)(2,1)} async-done(((bf16[16,1024]{1,0:T(8,128)(2,1)}), bf16[1024,1024]{1,0:T(8,128)(2,1)}) %all-gather.2.cloned.1.call-update) | async-done | bytes 2097168 | tf_op jit(solution)/shard_map/all_gather | solution.py:18
  384.1 3.0 fusion.49
  387.1 2.3 copy.166
  389.3 4.0 bitcast_reduce_fusion
  393.4 2.9 fusion.1
  396.3 2.3 copy.167
  398.6 4.4 fusion.11
  403.0 1.8 gather_fusion.1
  404.7 1.7 bitcast_reduce_fusion.1
  406.5 1.6 copy.147
  408.0 1.8 gather_fusion.3
  409.8 1.2 fusion.18
  411.3 1.3 convolution_bitcast_fusion
  412.7 2.2 fusion.16
  415.1 2.7 copy.155
  417.8 1.3 convolution_convert_fusion
  419.2 34.7 %all_to_all.37 = bf16[8,256,512]{2,1,0:T(8,128)(2,1)S(1)} all-to-all(bf16[8,256,512]{2,1,0:T(8,128)(2,1)S(1)} %bitcast.134), channel_id=1, replica_groups=mesh['ctx_0'=4,'ctx_1'=16,'head'=8] {'head'}, dimensions={0} | all-to-all | bytes 4194304 | tf_op jit(solution)/shard_map/all_to_all | solution.py:63
  454.0 1.0 reduce_sum.74
  (59 shorter events, 8.9 us)
Async XLA Ops:
  6.5 38.7 %copy-start.4 = (bf16[512,64]{0,1:T(8,128)(2,1)S(1)}, bf16[512,64]{0,1:T(8,128)(2,1)}, u32[]{:S(2)}) copy-start(bf16[512,64]{0,1:T(8,128)(2,1)} %param.16) | copy-start | bytes 196612
  19.0 26.3 %all-to-all-start.1 = ((s32[4,16,1,1,2]{0,4,3,2,1:T(2,128)}), s32[4,16,1,1,2]{0,4,3,2,1:T(2,128)S(1)}, u32[]{:S(2)}, u32[]{:S(2)}) async-start(s32[4,16,1,1,2]{0,4,3,2,1:T(2,128)} %copy.139), calls=%async_computation.1 | async-start | bytes 32768 | tf_op jit(solution)/shard_map/all_to_all | solution.py:36
  33.9 25.7 %copy-start.1 = (bf16[1024,512]{1,0:T(8,128)(2,1)S(1)}, bf16[1024,512]{1,0:T(8,128)(2,1)}, u32[]{:S(2)}) copy-start(bf16[1024,512]{1,0:T(8,128)(2,1)} %param.13) | copy-start | bytes 3145732
  46.0 8.9 %all-to-all-start.4 = ((bf16[4,1,512,64]{2,3,1,0:T(8,128)(2,1)}), bf16[4,1,512,64]{2,3,1,0:T(8,128)(2,1)S(1)}, u32[]{:S(2)}, u32[]{:S(2)}) async-start(bf16[4,1,512,64]{2,3,1,0:T(8,128)(2,1)} %stack.10), calls=%async_computation.4 | async-start | bytes 524288 | tf_op jit(solution)/shard_map/all_to_all | solution.py:49
  54.9 50.8 %all-to-all-start.2 = ((bf16[64,1,64,128]{3,2,1,0:T(8,128)(2,1)}), bf16[64,1,64,128]{3,2,1,0:T(8,128)(2,1)S(1)}, u32[]{:S(2)}, u32[]{:S(2)}) async-start(bf16[64,1,64,128]{3,2,1,0:T(8,128)(2,1)} %bitcast.12), calls=%async_computation.2 | async-start | bytes 2097152 | tf_op jit(solution)/shard_map/all_to_all | solution.py:129
  167.3 9.3 %copy-start.5 = (bf16[16,512]{1,0:T(8,128)(2,1)S(1)}, bf16[16,512]{1,0:T(8,128)(2,1)}, u32[]{:S(2)}) copy-start(bf16[16,512]{1,0:T(8,128)(2,1)} %param.15) | copy-start | bytes 49156
  167.3 9.3 %copy-start.6 = (bf16[16,512]{1,0:T(8,128)(2,1)S(1)}, bf16[16,512]{1,0:T(8,128)(2,1)}, u32[]{:S(2)}) copy-start(bf16[16,512]{1,0:T(8,128)(2,1)} %param.14) | copy-start | bytes 49156
  167.3 10.2 %copy-start = (bf16[256,512]{1,0:T(8,128)(2,1)S(1)}, bf16[256,512]{1,0:T(8,128)(2,1)}, u32[]{:S(2)}) copy-start(bf16[256,512]{1,0:T(8,128)(2,1)} %param.9) | copy-start | bytes 786436
  167.3 10.3 %copy-start.3 = (bf16[256,512]{1,0:T(8,128)(2,1)S(1)}, bf16[256,512]{1,0:T(8,128)(2,1)}, u32[]{:S(2)}) copy-start(bf16[256,512]{1,0:T(8,128)(2,1)} %param.10) | copy-start | bytes 786436
  167.3 247.8 %all-to-all-start.5 = ((bf16[16,4,512,64]{2,3,1,0:T(8,128)(2,1)}), bf16[16,4,512,64]{2,3,1,0:T(8,128)(2,1)}, u32[]{:S(2)}, u32[]{:S(2)}) async-start(bf16[16,4,512,64]{2,3,1,0:T(8,128)(2,1)} %stack.11), calls=%async_computation.5 | async-start | bytes 8388608 | tf_op jit(solution)/shard_map/all_to_all | solution.py:49
  176.4 207.7 %all-gather.2.cloned.1.call-start = ((), (), s32[]{:S(2)}) async-start(), calls=%async_computation.7 | async-start | bytes 2129920 | tf_op jit(solution)/shard_map/all_gather | solution.py:18
  177.5 211.8 %copy-start.2 = (bf16[4,64,4,128]{3,2,1,0:T(4,128)(2,1)}, bf16[4,64,4,128]{3,2,1,0:T(4,128)(2,1)S(1)}, u32[]{:S(2)}) copy-start(bf16[4,64,4,128]{3,2,1,0:T(4,128)(2,1)S(1)} %reshape_reshape.11) | copy-start | bytes 786436
Sparse Core Ops, SparseCore 0:
  180.1 203.8 all-gather.1
